TPU v7x, 32 devices: a whole 2x2x4 slice. The times are simulated.
32 devices in a mesh: groups: 2 (over y), cache: 4 (over z), blk: 4 (over x, core).
Axes of the slice: x: 2, y: 2, z: 4, core: 2. Of those that a mesh axis runs over, the one named last changes fastest.
Arguments:
- queries: bfloat16 [8, 512, 2048], P(('groups', 'cache'), 'blk'), parts along dimension 0, may hold values from -6 to 6
- kv_new: bfloat16 [8, 512, 1024], P(('groups', 'cache'), 'blk'), parts along dimension 0, may hold values from -6 to 6
- page_pool: bfloat16 [8, 128, 8, 1024], P(('groups', 'cache')), parts along dimension 0, may hold values from -6 to 6
- page_owner: int32 [8, 4, 32, 1], P(('groups', 'cache'), 'blk'), parts along dimension 0, may hold values from 0 to 3; in each aligned block of 32 rows (0 to 31, 32 to 63, ..., all dimensions but the last counted through in order) at most 16 rows name the same one
- page_slot: int32 [8, 4, 32], P(('groups', 'cache'), 'blk'), parts along dimension 0, may hold values from 0 to 127
- prefix_len: int32 [8], P(('groups', 'cache')), parts along dimension 0, may hold values from 1 to 1024, 2048 in all
- suffix_len: int32 [8], P(('groups', 'cache')), parts along dimension 0, may hold values from 1 to 512, 1536 in all
- ssm_in: bfloat16 [8, 512, 2048], P(('groups', 'cache'), 'blk'), parts along dimension 0, may hold values from -6 to 6
- b_in: bfloat16 [8, 512, 128], P(('groups', 'cache'), 'blk'), parts along dimension 0, may hold values from -4 to 4
- c_in: bfloat16 [8, 512, 128], P(('groups', 'cache'), 'blk'), parts along dimension 0, may hold values from -4 to 4
- step_size: float32 [8, 512, 32], P(('groups', 'cache'), 'blk'), parts along dimension 0, may hold values from 0.01 to 0.1
- decay_rate: float32 [32], replicated, may hold values from 0.001953125 to 4
- skip_gain: float32 [32], replicated, may hold values from 0.5 to 1.5
- prior_state: float32 [8, 32, 64, 128], P(('groups', 'cache')), parts along dimension 0, may hold values from -4 to 4
Outputs:
- attn_out: bfloat16 [8, 512, 2048], P(('groups', 'cache'), 'blk'), parts along dimension 0
- ssm_out: bfloat16 [8, 512, 2048], P(('groups', 'cache'), 'blk'), parts along dimension 0
There are 2 independent parts, one for each index of `groups`. A program takes and returns all parts, laid end to end along the dimension named above; an argument that names none is the same for every part. Nothing has to cross between parts.
Inputs may be any that keep to these rules, and one draw needn't show every extreme that they name: `page_owner`: among the 32 pages of one request at one index of blk, no owner is named more than 16 times, a bound that some block reaches. `prefix_len`: the largest is 1024. `suffix_len`: the largest is 512.
All inputs are finite; a program needn't handle non-finite values. No bound on the sum of `prefix_len` or of `suffix_len` on one device may be relied on, other than what follows from the above.
Results may differ from a plain program's by a relative error of at most 0.008.
Values may be sent and summed in bfloat16 or wider, within the bound.
A program may use at most 128 MiB of HBM per device.

v0:
```python
import math

import jax
import jax.numpy as jnp
from jax import lax
from jax.sharding import PartitionSpec as P

QH = 16
KVH = 4
HD = 128
SH = 32
HP = 64
NS = 128
PAGE = 8
LIST = 32


NEG = -1e30


def passed_along(value, axis, steps):
    count = lax.axis_size(axis)
    leading, last = (max(0, -steps), min(count, count - steps))
    return lax.ppermute(value, axis, [(source, source + steps) for source in range(leading, last)])


def for_sending(shard):

    def short(part):
        return part.astype(jnp.bfloat16) if part.dtype == jnp.float32 else part

    return jax.tree.map(short, shard)


def attend(carry, grouped, block_rows, visible):
    biggest, totals, accum = carry
    count = block_rows.shape[0]
    half = block_rows.shape[1] // 2
    keys_part = block_rows[:, :half].reshape(count, KVH, HD)
    values_part = block_rows[:, half:].reshape(count, KVH, HD)
    scores = jnp.einsum(
        "qhgd,khd->hgqk", grouped, keys_part, preferred_element_type=jnp.float32
    ) * (1.0 / math.sqrt(HD))
    masked = jnp.where(visible[None, None], scores, NEG)
    renewed = jnp.maximum(biggest, jnp.max(masked, axis=-1))
    weights = jnp.where(visible[None, None], jnp.exp(scores - renewed[..., None]), 0.0)
    factor = jnp.exp(biggest - renewed)
    totals = totals * factor + jnp.sum(weights, axis=-1)
    accum = accum * factor[..., None] + jnp.einsum(
        "hgqk,khd->hgqd",
        weights.astype(jnp.bfloat16),
        values_part,
        preferred_element_type=jnp.float32,
    )
    return (renewed, totals, accum)


def fetch_pages(owner_list, slot_list, pool_pages, capacity):
    owners_count = lax.axis_size("cache")
    onehot = (owner_list[:, None] == jnp.arange(owners_count, dtype=jnp.int32)[None, :]).astype(
        jnp.int32
    )
    earlier = jnp.cumsum(onehot, axis=0) - onehot
    ranking = jnp.sum(earlier * onehot, axis=1)
    wanted_slots = (
        jnp.zeros((owners_count, capacity), jnp.int32).at[owner_list, ranking].set(slot_list)
    )
    arrived = lax.all_to_all(
        pool_pages[lax.all_to_all(wanted_slots, "cache", split_axis=0, concat_axis=0, tiled=True)],
        "cache",
        split_axis=0,
        concat_axis=0,
        tiled=True,
    )
    return arrived[owner_list, ranking]


def combine(earlier, later):
    return (earlier[0] * later[0], later[0][:, None, None] * earlier[1] + later[1])


def local(
    queries,
    kv_new,
    page_pool,
    page_owner,
    page_slot,
    prefix_len,
    suffix_len,
    ssm_in,
    b_in,
    c_in,
    step_size,
    decay_rate,
    skip_gain,
    prior_state,
):
    blocks = lax.axis_size("blk")
    position_here = lax.axis_index("blk")
    tokens = queries.shape[1]
    kv_width = kv_new.shape[2]
    group = QH // KVH
    prefix_limit = prefix_len[0]
    suffix_limit = suffix_len[0]
    local_positions = jnp.arange(tokens, dtype=jnp.int32)
    query_positions = position_here * tokens + local_positions
    grouped = queries[0].reshape(tokens, KVH, group, HD)
    carry = (
        jnp.full((KVH, group, tokens), NEG, jnp.float32),
        jnp.zeros((KVH, group, tokens), jnp.float32),
        jnp.zeros((KVH, group, tokens, HD), jnp.float32),
    )
    pool_pages = page_pool[0]
    capacity = max(2, 2 * LIST // lax.axis_size("cache"))
    all_owners, all_slots = (
        lax.all_gather(page_owner[:, :, :, 0], "blk", axis=1, tiled=True),
        lax.all_gather(page_slot, "blk", axis=1, tiled=True),
    )
    fetched = fetch_pages(
        all_owners[0].reshape(-1), all_slots[0].reshape(-1), pool_pages, capacity * blocks
    )
    page_rows = fetched.reshape(-1, kv_width)
    block_ids = jnp.arange(blocks, dtype=jnp.int32)[:, None, None]
    item_ids = jnp.arange(LIST, dtype=jnp.int32)[None, :, None]
    offsets = jnp.arange(PAGE, dtype=jnp.int32)[None, None, :]
    page_positions = ((item_ids * blocks + block_ids) * PAGE + offsets).reshape(-1)
    valid = page_positions < prefix_limit
    total = page_rows.shape[0]
    width = 512

    def page_block(index, state):
        rows_block = lax.dynamic_slice_in_dim(page_rows, index * width, width, 0)
        seen = lax.dynamic_slice_in_dim(valid, index * width, width, 0)
        return attend(state, grouped, rows_block, jnp.broadcast_to(seen[None, :], (tokens, width)))

    carry = lax.fori_loop(0, total // width, page_block, carry)
    suffix_rows = kv_new[0]
    for step in range(blocks):
        if step > 0:
            suffix_rows = passed_along(suffix_rows, "blk", 1)
        anchor = (position_here - step) % blocks
        key_positions = anchor * tokens + local_positions
        carry = attend(
            carry,
            grouped,
            suffix_rows,
            (key_positions[None, :] <= query_positions[:, None])
            & (key_positions[None, :] < suffix_limit),
        )
    biggest, totals, accum = carry
    mixed = jnp.transpose(accum / totals[..., None], (2, 0, 1, 3)).reshape(tokens, QH * HD)
    attn_out = jnp.where((query_positions < suffix_limit)[:, None], mixed, 0.0).astype(
        jnp.bfloat16
    )[None]
    inputs = ssm_in[0].reshape(tokens, SH, HP)
    b_rows = b_in[0]
    c_rows = c_in[0]
    steps_dt = step_size[0]
    logs = jnp.cumsum(-steps_dt * decay_rate[None, :], axis=0)
    last = logs[-1]
    gram = jnp.dot(c_rows, b_rows.T, preferred_element_type=jnp.float32)
    lower = local_positions[:, None] >= local_positions[None, :]
    exponent = jnp.where(lower[None], logs.T[:, :, None] - logs.T[:, None, :], NEG)
    mixing = (gram[None] * jnp.exp(exponent) * steps_dt.T[:, None, :]).astype(jnp.bfloat16)
    inner = jnp.einsum("hts,shp->thp", mixing, inputs, preferred_element_type=jnp.float32)
    scaled = (
        (jnp.exp(last[None, :] - logs) * steps_dt)[:, :, None] * inputs.astype(jnp.float32)
    ).astype(jnp.bfloat16)
    local_state = jnp.einsum("shp,sn->hpn", scaled, b_rows, preferred_element_type=jnp.float32)
    local_decay = jnp.exp(last)
    identity = (jnp.ones((SH,), jnp.float32), jnp.zeros((SH, HP, NS), jnp.float32))
    prefix_decay, prefix_state = identity
    for round_index in range(blocks - 1):
        outgoing = combine((prefix_decay, prefix_state), (local_decay, local_state))
        incoming = passed_along((for_sending(outgoing[0]), for_sending(outgoing[1])), "blk", 1)
        prefix_decay = jnp.where(position_here == 0, identity[0], incoming[0])
        prefix_state = jnp.where(position_here == 0, identity[1], incoming[1])
    entering = prefix_decay[:, None, None] * prior_state[0] + prefix_state
    carried = jnp.exp(logs)[:, :, None] * jnp.einsum(
        "tn,hpn->thp", c_rows.astype(jnp.float32), entering, precision=lax.Precision.HIGHEST
    )
    result = inner + carried + skip_gain[None, :, None] * inputs.astype(jnp.float32)
    result = jnp.where((query_positions < suffix_limit)[:, None, None], result, 0.0)
    ssm_out = result.reshape(tokens, SH * HP).astype(jnp.bfloat16)[None]
    return (attn_out, ssm_out)


def solution(mesh):
    in_specs = (
        P(("groups", "cache"), "blk", None),
        P(("groups", "cache"), "blk", None),
        P(("groups", "cache"), None, None, None),
        P(("groups", "cache"), "blk", None, None),
        P(("groups", "cache"), "blk", None),
        P(("groups", "cache")),
        P(("groups", "cache")),
        P(("groups", "cache"), "blk", None),
        P(("groups", "cache"), "blk", None),
        P(("groups", "cache"), "blk", None),
        P(("groups", "cache"), "blk", None),
        P(),
        P(),
        P(("groups", "cache"), None, None, None),
    )
    out_specs = (P(("groups", "cache"), "blk", None), P(("groups", "cache"), "blk", None))
    return jax.shard_map(local, mesh=mesh, in_specs=in_specs, out_specs=out_specs, check_vma=False)
```

profile of v0, /device:TPU:0, one launch (start us, length us, event | category | flops | bytes accessed | tf_op | source)
XLA Modules:
  0.0 198.7 jit_solution(4039296911272048753)
XLA Ops:
  0.6 6.3 %all-gather = s32[1,4,32,1]{2,3,0,1:T(1,128)S(1)} all-gather(s32[1,1,32,1]{2,3,0,1:T(1,128)} %bitcast.279), channel_id=2, replica_groups=mesh['groups'=2,'cache'=4,'blk'=4] {'blk'}, dimensions={1}, use_global_device_ids=true | all-gather | bytes 640 | tf_op jit(solution)/shard_map/all_gather | solution.py:116
  8.7 5.4 %all_gather.7 = s32[1,4,32]{2,0,1:T(1,128)S(1)} all-gather(s32[1,1,32]{2,0,1:T(1,128)} %bitcast.280), channel_id=1, replica_groups=mesh['groups'=2,'cache'=4,'blk'=4] {'blk'}, dimensions={1}, use_global_device_ids=true | all-gather | bytes 640 | tf_op jit(solution)/shard_map/all_gather | solution.py:117
  15.4 19.7 %scatter_fusion = s32[4,64]{1,0:T(4,128)} fusion(s32[4,64]{1,0:T(4,128)} %broadcast.351, s32[128]{0:T(128)S(1)} %get-tuple-element.209, s32[128]{0:T(128)S(1)} %reshape.502), kind=kCustom, calls=%fused_computation.2 | custom fusion | bytes 2560 | tf_op jit(solution)/shard_map/scatter | solution.py:66
  35.1 5.1 %all-to-all-start = ((s32[4,1,64]{2,1,0:T(1,128)}), s32[4,1,64]{2,1,0:T(1,128)S(1)}, u32[]{:S(2)}, u32[]{:S(2)}) async-start(s32[4,1,64]{2,1,0:T(1,128)} %bitcast.8), calls=%async_computation | async-start | bytes 4096 | tf_op jit(solution)/shard_map/all_to_all | solution.py:69
  41.4 2.6 %collective-permute-start = (bf16[128,1024]{0,1:T(8,128)(2,1)S(1)}, bf16[128,1024]{0,1:T(8,128)(2,1)}, u32[]{:S(2)}, u32[]{:S(2)}) collective-permute-start(bf16[128,1024]{0,1:T(8,128)(2,1)S(1)} %bitcast.243), channel_id=1, source_target_pairs={{0,1},{1,2},{2,3},{4,5},{5,6},{6,7},{8,9},{9,10},{10,11},{12,13},{... | collective-permute-start | bytes 786440 | tf_op jit(solution)/shard_map/ppermute | solution.py:24
  46.3 3.3 %collective-permute-start.3 = (bf16[32]{0:T(256)(128)(2,1)}, bf16[32]{0:T(256)(128)(2,1)}, u32[]{:S(2)}, u32[]{:S(2)}) collective-permute-start(bf16[32]{0:T(256)(128)(2,1)} %fusion.89), channel_id=1, source_target_pairs={{0,1},{1,2},{2,3},{4,5},{5,6},{6,7},{8,9},{9,10},{10,11},{12,13},{... | collective-permute-start | bytes 200 | tf_op jit(solution)/shard_map/ppermute | solution.py:24
  49.7 2.8 %gather_fusion = bf16[256,8,1024]{2,1,0:T(8,128)(2,1)} fusion(bf16[128,8,1024]{2,1,0:T(8,128)(2,1)S(1)} %bitcast.226, s32[1024]{0:T(1024)S(1)} %pad_clamp_fusion), kind=kCustom, calls=%fused_computation | custom fusion | bytes 8389632 | tf_op jit(solution)/shard_map/gather | solution.py:69
  52.5 5.2 %all-to-all-start.1 = ((bf16[4,64,8,1024]{3,2,1,0:T(8,128)(2,1)}), bf16[4,64,8,1024]{3,2,1,0:T(8,128)(2,1)}, u32[]{:S(2)}, u32[]{:S(2)}) async-start(bf16[4,64,8,1024]{3,2,1,0:T(8,128)(2,1)} %bitcast.234), calls=%async_computation.1 | async-start | bytes 8388608 | tf_op jit(solution)/shard_map/all_to_all | solution.py:68
  65.7 2.7 %convolution_bitcast_fusion.1 = f32[128,32,64]{0,2,1:T(8,128)} fusion(bf16[128,32,64]{0,2,1:T(8,128)(2,1)S(1)} %bitcast.237, f32[32,128]{1,0:T(8,128)} %bitcast.276, f32[32,128]{1,0:T(8,128)} %copy.119, f32[128,128]{1,0:T(8,128)S(1)} %fusion.73, pred[128,128]{1,0:T(8,128)(4,1)S(1)} %iota_compare_fusion), kind=kOutput, calls=%fused_computation.46 | convolution fusion | flops 69730304 | bytes 1687552 | tf_op jit(solution)/shard_map/hts,shp->thp/dot_general | solution.py:165
  68.4 2.0 %select_reduce_fusion.3 = (f32[4,4,128]{2,1,0:T(4,128)}, f32[4,4,128,128]{2,3,1,0:T(8,128)}) fusion(pred[128,128]{0,1:T(8,128)(4,1)S(1)} %get-tuple-element.228, bf16[128,4,128,1]{0,2,3,1:T(8,128)(2,1)S(1)} %bitcast.251, bf16[128,4,4,128]{0,3,2,1:T(8,128)(2,1)S(1)} %bitcast.229), kind=kOutput, calls=%fused_computation.70 | convolution fusion | flops 67893248 | bytes 1728512 | tf_op jit(solution)/shard_map/qhgd,khd->hgqk/dot_general | solution.py:41
  75.5 3.0 %collective-permute-start.6 = (bf16[32,64,128]{2,1,0:T(8,128)(2,1)}, bf16[32,64,128]{2,1,0:T(8,128)(2,1)}, u32[]{:S(2)}, u32[]{:S(2)}) collective-permute-start(bf16[32,64,128]{2,1,0:T(8,128)(2,1)} %get-tuple-element.240), channel_id=1, source_target_pairs={{0,1},{1,2},{2,3},{4,5},{5,6},{6,7},{8,9},{9,10},{10,11},{12,13},{... | collective-permute-start | bytes 1572872 | tf_op jit(solution)/shard_map/ppermute | solution.py:24
  80.3 3.1 %collective-permute-start.5 = (bf16[32]{0:T(256)(128)(2,1)S(1)}, bf16[32]{0:T(256)(128)(2,1)S(1)}, u32[]{:S(2)}, u32[]{:S(2)}) collective-permute-start(bf16[32]{0:T(256)(128)(2,1)S(1)} %get-tuple-element.225), channel_id=1, source_target_pairs={{0,1},{1,2},{2,3},{4,5},{5,6},{6,7},{8,9},{9,10},{10,11},{12,13},{... | collective-permute-start | bytes 200 | tf_op jit(solution)/shard_map/ppermute | solution.py:24
  83.4 1.5 copy.123
  85.0 3.1 %collective-permute-start.1 = (bf16[128,1024]{0,1:T(8,128)(2,1)}, bf16[128,1024]{0,1:T(8,128)(2,1)S(1)}, u32[]{:S(2)}, u32[]{:S(2)}) collective-permute-start(bf16[128,1024]{0,1:T(8,128)(2,1)} %collective-permute-done), channel_id=1, source_target_pairs={{0,1},{1,2},{2,3},{4,5},{5,6},{6,7},{8,9},{9,10},{10,11},{12,13},{... | collective-permute-start | bytes 786440 | tf_op jit(solution)/shard_map/ppermute | solution.py:24
  88.0 1.6 add_convert_fusion.1
  89.6 4.4 %collective-permute-start.7 = (bf16[32,64,128]{2,1,0:T(8,128)(2,1)S(1)}, bf16[32,64,128]{2,1,0:T(8,128)(2,1)S(1)}, u32[]{:S(2)}, u32[]{:S(2)}) collective-permute-start(bf16[32,64,128]{2,1,0:T(8,128)(2,1)S(1)} %add_convert_fusion.1), channel_id=1, source_target_pairs={{0,1},{1,2},{2,3},{4,5},{5,6},{6,7},{8,9},{9,10},{10,11},{12,13},{... | collective-permute-start | bytes 1572872 | tf_op jit(solution)/shard_map/ppermute | solution.py:24
  95.1 1.9 select_reduce_fusion.2
  97.0 1.9 collective-permute-start.2
  99.8 3.2 %collective-permute-start.8 = (bf16[32,64,128]{2,1,0:T(8,128)(2,1)S(1)}, bf16[32,64,128]{2,1,0:T(8,128)(2,1)S(1)}, u32[]{:S(2)}, u32[]{:S(2)}) collective-permute-start(bf16[32,64,128]{2,1,0:T(8,128)(2,1)S(1)} %add_convert_fusion), channel_id=1, source_target_pairs={{0,1},{1,2},{2,3},{4,5},{5,6},{6,7},{8,9},{9,10},{10,11},{12,13},{... | collective-permute-start | bytes 1572872 | tf_op jit(solution)/shard_map/ppermute | solution.py:24
  103.0 2.6 %select_reduce_fusion.1 = (f32[4,4,128]{2,1,0:T(4,128)}, f32[4,4,128,128]{2,3,1,0:T(8,128)}) fusion(pred[128,128]{0,1:T(8,128)(4,1)} %get-tuple-element.229, bf16[128,4,128,1]{0,2,3,1:T(8,128)(2,1)S(1)} %bitcast.250, bf16[128,4,4,128]{0,3,2,1:T(8,128)(2,1)S(1)} %bitcast.232), kind=kOutput, calls=%fused_computation.66 | convolution fusion | flops 67893248 | bytes 1728512 | tf_op jit(solution)/shard_map/qhgd,khd->hgqk/dot_general | solution.py:41
  106.4 2.0 select_reduce_fusion
  110.3 40.6 %all-to-all-done.1 = bf16[4,64,8,1024]{3,2,1,0:T(8,128)(2,1)} async-done(((bf16[4,64,8,1024]{3,2,1,0:T(8,128)(2,1)}), bf16[4,64,8,1024]{3,2,1,0:T(8,128)(2,1)}, u32[]{:S(2)}, u32[]{:S(2)}) %all-to-all-start.1) | async-done | bytes 4194336 | tf_op jit(solution)/shard_map/all_to_all | solution.py:68
  150.9 4.4 %gather_fusion.1 = bf16[128,8,1024]{2,1,0:T(8,128)(2,1)} fusion(bf16[4,64,8,1024]{3,2,1,0:T(8,128)(2,1)} %all-to-all-done.1, s32[128]{0:T(128)S(1)} %bitcast.236), kind=kCustom, calls=%fused_computation.1 | custom fusion | bytes 4195328 | tf_op jit(solution)/shard_map/gather | solution.py:75
  155.3 31.0 %while.18 = (s32[]{:T(128)}, f32[4,4,128]{2,1,0:T(4,128)S(1)}, f32[4,4,128]{2,1,0:T(4,128)}, f32[4,4,128,128]{3,2,1,0:T(8,128)}, pred[1024]{0:T(1024)(128)(4,1)S...) while((s32[]{:T(128)}, f32[4,4,128]{2,1,0:T(4,128)S(1)}, ...), condition=%wide.region_6.7_spmd.clone, body=%wide.region_3.6_spmd.clone.sunk | while | flops 549201920 | bytes 20581072 | solution.py:136
  157.7 4.2 %fusion.129 = (f32[4,4,128]{2,1,0:T(4,128)S(1)}, f32[4,512,128,4]{2,1,3,0:T(8,128)}) fusion(pred[512]{0:T(512)(128)(4,1)S(1)} %dynamic_slice.17, bf16[512,4,128,1]{0,2,3,1:T(8,128)(2,1)} %bitcast.227, bf16[128,4,4,128]{3,0,2,1:T(8,128)(2,1)} %get-tuple-element.344), kind=kOutput, calls=%fused_computation.5.clone.1 | convolution fusion | flops 271579136 | bytes 5251584 | tf_op jit(solution)/shard_map/while/body/eval_jaxpr/qhgd,khd->hgqk/dot_general | solution.py:41
  161.9 3.1 %fusion.130 = f32[4,4,128]{2,1,0:T(4,128)S(1)} fusion(f32[4,512,128,4]{2,1,3,0:T(8,128)} %get-tuple-element.310, f32[4,4,128]{2,1,0:T(4,128)S(1)} %select_maximum_fusion.2, pred[512]{0:T(512)(128)(4,1)S(1)} %dynamic_slice.17), kind=kLoop, calls=%fused_computation.9.clone.1 | loop fusion | flops 4192256 | bytes 4211200 | tf_op jit(solution)/shard_map/while/body/eval_jaxpr/reduce_sum | solution.py:48
  165.8 4.5 %fusion.132 = f32[4,4,128,128]{3,2,1,0:T(8,128)} fusion(bf16[512,4,128,1]{0,2,3,1:T(8,128)(2,1)S(1)} %bitcast.235, f32[4,512,128,4]{2,1,3,0:T(8,128)} %get-tuple-element.310, f32[4,4,128]{2,1,0:T(4,128)S(1)} %select_maximum_fusion.2, pred[512]{0:T(512)(128)(4,1)S(1)} %dynamic_slice.17, f32[4,4,128,128]{3,2,1,0:T(8,128)} %get-tuple-element.329, ...), kind=kOutput, calls=%fused_computation.15.clone.1 | convolution fusion | flops 273416192 | bytes 6832641 | tf_op jit(solution)/shard_map/while/body/eval_jaxpr/hgqk,khd->hgqd/dot_general | solution.py:49
  172.7 4.2 %fusion.129 = (f32[4,4,128]{2,1,0:T(4,128)S(1)}, f32[4,512,128,4]{2,1,3,0:T(8,128)}) fusion(pred[512]{0:T(512)(128)(4,1)S(1)} %dynamic_slice.17, bf16[512,4,128,1]{0,2,3,1:T(8,128)(2,1)} %bitcast.227, bf16[128,4,4,128]{3,0,2,1:T(8,128)(2,1)} %get-tuple-element.344), kind=kOutput, calls=%fused_computation.5.clone.1 | convolution fusion | flops 271579136 | bytes 5251584 | tf_op jit(solution)/shard_map/while/body/eval_jaxpr/qhgd,khd->hgqk/dot_general | solution.py:41
  176.9 3.1 %fusion.130 = f32[4,4,128]{2,1,0:T(4,128)S(1)} fusion(f32[4,512,128,4]{2,1,3,0:T(8,128)} %get-tuple-element.310, f32[4,4,128]{2,1,0:T(4,128)S(1)} %select_maximum_fusion.2, pred[512]{0:T(512)(128)(4,1)S(1)} %dynamic_slice.17), kind=kLoop, calls=%fused_computation.9.clone.1 | loop fusion | flops 4192256 | bytes 4211200 | tf_op jit(solution)/shard_map/while/body/eval_jaxpr/reduce_sum | solution.py:48
  181.5 4.8 %fusion.132 = f32[4,4,128,128]{3,2,1,0:T(8,128)} fusion(bf16[512,4,128,1]{0,2,3,1:T(8,128)(2,1)S(1)} %bitcast.235, f32[4,512,128,4]{2,1,3,0:T(8,128)} %get-tuple-element.310, f32[4,4,128]{2,1,0:T(4,128)S(1)} %select_maximum_fusion.2, pred[512]{0:T(512)(128)(4,1)S(1)} %dynamic_slice.17, f32[4,4,128,128]{3,2,1,0:T(8,128)} %get-tuple-element.329, ...), kind=kOutput, calls=%fused_computation.15.clone.1 | convolution fusion | flops 273416192 | bytes 6832641 | tf_op jit(solution)/shard_map/while/body/eval_jaxpr/hgqk,khd->hgqd/dot_general | solution.py:49
  186.3 2.7 %copy.106 = f32[4,4,128,128]{2,3,1,0:T(8,128)} copy(f32[4,4,128,128]{3,2,1,0:T(8,128)} %get-tuple-element.128) | data formatting | bytes 2097152 | tf_op jit(solution)/shard_map/while | solution.py:136
  192.8 1.4 fusion.43
  (144 shorter events, 39.8 us)
Async XLA Ops:
  0.6 49.0 %copy-start = (bf16[1,128,8,1024]{3,2,1,0:T(8,128)(2,1)S(1)}, bf16[1,128,8,1024]{3,2,1,0:T(8,128)(2,1)}, u32[]{:S(2)}) copy-start(bf16[1,128,8,1024]{3,2,1,0:T(8,128)(2,1)} %param.18) | copy-start | bytes 6291460
  35.1 14.4 %all-to-all-start = ((s32[4,1,64]{2,1,0:T(1,128)}), s32[4,1,64]{2,1,0:T(1,128)S(1)}, u32[]{:S(2)}, u32[]{:S(2)}) async-start(s32[4,1,64]{2,1,0:T(1,128)} %bitcast.8), calls=%async_computation | async-start | bytes 4096 | tf_op jit(solution)/shard_map/all_to_all | solution.py:69
  41.4 43.6 %collective-permute-start = (bf16[128,1024]{0,1:T(8,128)(2,1)S(1)}, bf16[128,1024]{0,1:T(8,128)(2,1)}, u32[]{:S(2)}, u32[]{:S(2)}) collective-permute-start(bf16[128,1024]{0,1:T(8,128)(2,1)S(1)} %bitcast.243), channel_id=1, source_target_pairs={{0,1},{1,2},{2,3},{4,5},{5,6},{6,7},{8,9},{9,10},{10,11},{12,13},{... | collective-permute-start | bytes 786440 | tf_op jit(solution)/shard_map/ppermute | solution.py:24
  46.3 25.0 %collective-permute-start.3 = (bf16[32]{0:T(256)(128)(2,1)}, bf16[32]{0:T(256)(128)(2,1)}, u32[]{:S(2)}, u32[]{:S(2)}) collective-permute-start(bf16[32]{0:T(256)(128)(2,1)} %fusion.89), channel_id=1, source_target_pairs={{0,1},{1,2},{2,3},{4,5},{5,6},{6,7},{8,9},{9,10},{10,11},{12,13},{... | collective-permute-start | bytes 200 | tf_op jit(solution)/shard_map/ppermute | solution.py:24
  52.5 6.4 %copy-start.9 = (bf16[1,128,2048]{2,1,0:T(8,128)(2,1)S(1)}, bf16[1,128,2048]{2,1,0:T(8,128)(2,1)}, u32[]{:S(2)}) copy-start(bf16[1,128,2048]{2,1,0:T(8,128)(2,1)} %param.16) | copy-start | bytes 1572868
  52.5 98.4 %all-to-all-start.1 = ((bf16[4,64,8,1024]{3,2,1,0:T(8,128)(2,1)}), bf16[4,64,8,1024]{3,2,1,0:T(8,128)(2,1)}, u32[]{:S(2)}, u32[]{:S(2)}) async-start(bf16[4,64,8,1024]{3,2,1,0:T(8,128)(2,1)} %bitcast.234), calls=%async_computation.1 | async-start | bytes 8388608 | tf_op jit(solution)/shard_map/all_to_all | solution.py:68
  63.4 7.0 %copy-start.14 = (pred[128,128]{0,1:T(8,128)(4,1)}, pred[128,128]{0,1:T(8,128)(4,1)S(1)}, u32[]{:S(2)}) copy-start(pred[128,128]{0,1:T(8,128)(4,1)S(1)} %get-tuple-element.228) | copy-start | bytes 49156
  65.0 9.0 %copy-start.18 = (bf16[1,128,128]{2,1,0:T(8,128)(2,1)S(1)}, bf16[1,128,128]{2,1,0:T(8,128)(2,1)}, u32[]{:S(2)}) copy-start(bf16[1,128,128]{2,1,0:T(8,128)(2,1)} %param.24) | copy-start | bytes 98308
  68.4 26.7 %copy-start.12 = (pred[128,128]{0,1:T(8,128)(4,1)S(1)}, pred[128,128]{0,1:T(8,128)(4,1)}, u32[]{:S(2)}) copy-start(pred[128,128]{0,1:T(8,128)(4,1)} %get-tuple-element.231) | copy-start | bytes 49156
  71.9 2.1 %collective-permute-start.4 = (bf16[32]{0:T(256)(128)(2,1)S(1)}, bf16[32]{0:T(256)(128)(2,1)S(1)}, u32[]{:S(2)}, u32[]{:S(2)}) collective-permute-start(bf16[32]{0:T(256)(128)(2,1)S(1)} %fusion.78), channel_id=1, source_target_pairs={{0,1},{1,2},{2,3},{4,5},{5,6},{6,7},{8,9},{9,10},{10,11},{12,13},{... | collective-permute-start | bytes 200 | tf_op jit(solution)/shard_map/ppermute | solution.py:24
  74.0 23.0 %copy-start.22 = (f32[32]{0:T(128)}, f32[32]{0:T(128)S(1)}, u32[]{:S(2)}) copy-start(f32[32]{0:T(128)S(1)} %get-tuple-element.227) | copy-start | bytes 388
  75.5 12.6 %collective-permute-start.6 = (bf16[32,64,128]{2,1,0:T(8,128)(2,1)}, bf16[32,64,128]{2,1,0:T(8,128)(2,1)}, u32[]{:S(2)}, u32[]{:S(2)}) collective-permute-start(bf16[32,64,128]{2,1,0:T(8,128)(2,1)} %get-tuple-element.240), channel_id=1, source_target_pairs={{0,1},{1,2},{2,3},{4,5},{5,6},{6,7},{8,9},{9,10},{10,11},{12,13},{... | collective-permute-start | bytes 1572872 | tf_op jit(solution)/shard_map/ppermute | solution.py:24
  78.6 29.7 %copy-start.23 = (pred[128]{0:T(512)(128)(4,1)}, pred[128]{0:T(512)(128)(4,1)S(1)}, u32[]{:S(2)}) copy-start(pred[128]{0:T(512)(128)(4,1)S(1)} %broadcast_compare_fusion.4) | copy-start | bytes 388
  80.3 4.6 %collective-permute-start.5 = (bf16[32]{0:T(256)(128)(2,1)S(1)}, bf16[32]{0:T(256)(128)(2,1)S(1)}, u32[]{:S(2)}, u32[]{:S(2)}) collective-permute-start(bf16[32]{0:T(256)(128)(2,1)S(1)} %get-tuple-element.225), channel_id=1, source_target_pairs={{0,1},{1,2},{2,3},{4,5},{5,6},{6,7},{8,9},{9,10},{10,11},{12,13},{... | collective-permute-start | bytes 200 | tf_op jit(solution)/shard_map/ppermute | solution.py:24
  84.9 14.0 %copy-start.4 = (f32[32,64,128]{2,1,0:T(8,128)S(1)}, f32[32,64,128]{2,1,0:T(8,128)}, u32[]{:S(2)}) copy-start(f32[32,64,128]{2,1,0:T(8,128)} %get-tuple-element.241) | copy-start | bytes 3145732
  85.0 12.1 %collective-permute-start.1 = (bf16[128,1024]{0,1:T(8,128)(2,1)}, bf16[128,1024]{0,1:T(8,128)(2,1)S(1)}, u32[]{:S(2)}, u32[]{:S(2)}) collective-permute-start(bf16[128,1024]{0,1:T(8,128)(2,1)} %collective-permute-done), channel_id=1, source_target_pairs={{0,1},{1,2},{2,3},{4,5},{5,6},{6,7},{8,9},{9,10},{10,11},{12,13},{... | collective-permute-start | bytes 786440 | tf_op jit(solution)/shard_map/ppermute | solution.py:24
  88.0 18.3 %copy-start.16 = (pred[128,128]{0,1:T(8,128)(4,1)S(1)}, pred[128,128]{0,1:T(8,128)(4,1)}, u32[]{:S(2)}) copy-start(pred[128,128]{0,1:T(8,128)(4,1)} %get-tuple-element.230) | copy-start | bytes 49156
  89.6 9.4 %collective-permute-start.7 = (bf16[32,64,128]{2,1,0:T(8,128)(2,1)S(1)}, bf16[32,64,128]{2,1,0:T(8,128)(2,1)S(1)}, u32[]{:S(2)}, u32[]{:S(2)}) collective-permute-start(bf16[32,64,128]{2,1,0:T(8,128)(2,1)S(1)} %add_convert_fusion.1), channel_id=1, source_target_pairs={{0,1},{1,2},{2,3},{4,5},{5,6},{6,7},{8,9},{9,10},{10,11},{12,13},{... | collective-permute-start | bytes 1572872 | tf_op jit(solution)/shard_map/ppermute | solution.py:24
  95.0 13.3 %copy-start.7 = (f32[1,32,64,128]{3,2,1,0:T(8,128)S(1)}, f32[1,32,64,128]{3,2,1,0:T(8,128)}, u32[]{:S(2)}) copy-start(f32[1,32,64,128]{3,2,1,0:T(8,128)} %param.29) | copy-start | bytes 3145732
  95.0 13.3 %copy-start.8 = (f32[128,32,64]{0,2,1:T(8,128)S(1)}, f32[128,32,64]{0,2,1:T(8,128)}, u32[]{:S(2)}) copy-start(f32[128,32,64]{0,2,1:T(8,128)} %convolution_bitcast_fusion.1) | copy-start | bytes 3145732
  95.0 13.3 %copy-start.19 = (bf16[1,128,128]{2,1,0:T(8,128)(2,1)S(1)}, bf16[1,128,128]{2,1,0:T(8,128)(2,1)}, u32[]{:S(2)}) copy-start(bf16[1,128,128]{2,1,0:T(8,128)(2,1)} %param.25) | copy-start | bytes 98308
  95.1 13.3 %copy-start.21 = (f32[128,32]{0,1:T(8,128)S(1)}, f32[128,32]{0,1:T(8,128)}, u32[]{:S(2)}) copy-start(f32[128,32]{0,1:T(8,128)} %copy.123) | copy-start | bytes 49156
  95.1 13.3 %copy-start.26 = (f32[32]{0:T(128)S(1)}, f32[32]{0:T(128)}, u32[]{:S(2)}) copy-start(f32[32]{0:T(128)} %param.28) | copy-start | bytes 388
  97.0 8.6 %collective-permute-start.2 = (bf16[128,1024]{0,1:T(8,128)(2,1)S(1)}, bf16[128,1024]{0,1:T(8,128)(2,1)S(1)}, u32[]{:S(2)}, u32[]{:S(2)}) collective-permute-start(bf16[128,1024]{0,1:T(8,128)(2,1)S(1)} %collective-permute-done.1), channel_id=1, source_target_pairs={{0,1},{1,2},{2,3},{4,5},{5,6},{6,7},{8,9},{9,10},{10,11},{12,13},{... | collective-permute-start | bytes 786440 | tf_op jit(solution)/shard_map/ppermute | solution.py:24
  99.8 8.6 %collective-permute-start.8 = (bf16[32,64,128]{2,1,0:T(8,128)(2,1)S(1)}, bf16[32,64,128]{2,1,0:T(8,128)(2,1)S(1)}, u32[]{:S(2)}, u32[]{:S(2)}) collective-permute-start(bf16[32,64,128]{2,1,0:T(8,128)(2,1)S(1)} %add_convert_fusion), channel_id=1, source_target_pairs={{0,1},{1,2},{2,3},{4,5},{5,6},{6,7},{8,9},{9,10},{10,11},{12,13},{... | collective-permute-start | bytes 1572872 | tf_op jit(solution)/shard_map/ppermute | solution.py:24
  108.3 47.0 %copy-start.25 = (pred[1024]{0:T(1024)(128)(4,1)S(1)}, pred[1024]{0:T(1024)(128)(4,1)}, u32[]{:S(2)}) copy-start(pred[1024]{0:T(1024)(128)(4,1)} %lt.128) | copy-start | bytes 3076
  186.3 7.9 %copy-start.1 = (f32[4,4,128,128]{2,3,1,0:T(8,128)S(1)}, f32[4,4,128,128]{2,3,1,0:T(8,128)}, u32[]{:S(2)}) copy-start(f32[4,4,128,128]{2,3,1,0:T(8,128)} %get-tuple-element.239) | copy-start | bytes 3145732
  186.3 9.7 %copy-start.10 = (bf16[128,512]{0,1:T(8,128)(2,1)S(1)}, bf16[128,512]{0,1:T(8,128)(2,1)}, u32[]{:S(2)}) copy-start(bf16[128,512]{0,1:T(8,128)(2,1)} %get-tuple-element.222) | copy-start | bytes 393220
  189.0 7.0 %copy-start.5 = (f32[4,4,128,128]{2,3,1,0:T(8,128)S(1)}, f32[4,4,128,128]{2,3,1,0:T(8,128)}, u32[]{:S(2)}) copy-start(f32[4,4,128,128]{2,3,1,0:T(8,128)} %copy.106) | copy-start | bytes 3145732
  189.0 7.0 %copy-start.15 = (pred[128,128]{0,1:T(8,128)(4,1)S(1)}, pred[128,128]{0,1:T(8,128)(4,1)}, u32[]{:S(2)}) copy-start(pred[128,128]{0,1:T(8,128)(4,1)} %copy-done.14) | copy-start | bytes 49156
  189.0 7.3 %copy-start.2 = (f32[4,4,128,128]{2,3,1,0:T(8,128)S(1)}, f32[4,4,128,128]{2,3,1,0:T(8,128)}, u32[]{:S(2)}) copy-start(f32[4,4,128,128]{2,3,1,0:T(8,128)} %get-tuple-element.237) | copy-start | bytes 3145732
  189.0 7.4 %copy-start.13 = (pred[128,128]{0,1:T(8,128)(4,1)S(1)}, pred[128,128]{0,1:T(8,128)(4,1)}, u32[]{:S(2)}) copy-start(pred[128,128]{0,1:T(8,128)(4,1)} %get-tuple-element.231) | copy-start | bytes 49156
  (6 other events, 9.7 us)
where the time goes:
time: 201 us; the launch traced here: 199 us
  local copies, waits for them, and re-layouts  48.4 us (24%)
  waiting for transfers between devices  41.3 us (21%)
  starting transfers between devices  36.3 us (18%)
  matrix products  33.4 us (17%)
  other arithmetic  25 us (12%)
  blocking collectives  11.7 us (6%)
  between operations  2.51 us (1%)
    all_to_all x1, waiting for transfers between devices, fetch_pages(): lax.all_to_all(pool_pages[lax.all_to_all(wanted_slots, 'cache', split_axi...  40.6 us
    ppermute x9, starting transfers between devices, passed_along(): lax.ppermute(value, axis, [(source, source + steps) for source in range(l...  25.9 us
    scatter x1, local copies, waits for them, and re-layouts, fetch_pages(): jnp.zeros((owners_count, capacity), jnp.int32).at[owner_list, ranking]  19.7 us
    dot_general x6, matrix products, attend(): jnp.einsum('qhgd,khd->hgqk', grouped, keys_part, preferred_element_type=j...  17 us
    reduce_sum x6, other arithmetic, attend(): totals = totals * factor + jnp.sum(weights, axis=-1)  11.4 us
    dot_general x6, matrix products, attend(): jnp.einsum('hgqk,khd->hgqd', weights.astype(jnp.bfloat16), values_part, p...  10.5 us
    all_gather x1, blocking collectives, local(): lax.all_gather(page_owner[:, :, :, 0], 'blk', axis=1, tiled=True)  6.28 us
    unnamed x60, local copies, waits for them, and re-layouts  5.84 us
  transfers between devices with their start and end apart: 11, of which 2 were waited for; matrix products, arithmetic and copies ran while one was open for 18% of the time, Pallas kernels for 0%

commit v1 on v0

v1 whole, which is shorter than its diff:
```python
import functools
import math

import jax
import jax.numpy as jnp
from jax import lax
from jax.experimental import pallas as pl
from jax.experimental.pallas import tpu as pltpu
from jax.sharding import PartitionSpec as P

QH = 16
KVH = 4
HD = 128
SH = 32
HP = 64
NS = 128
PAGE = 8
GROUP = QH // KVH
NEG = -1e30
F32 = jnp.float32
BF16 = jnp.bfloat16


def remote(src, dst, send_sem, recv_sem, device):
    return pltpu.make_async_remote_copy(
        src_ref=src,
        dst_ref=dst,
        send_sem=send_sem,
        recv_sem=recv_sem,
        device_id=device,
        device_id_type=pl.DeviceIdType.MESH,
    )


def nt(a, b, **kw):
    return lax.dot_general(a, b, (((1,), (1,)), ((), ())), preferred_element_type=F32, **kw)


def nn(a, b, **kw):
    return jnp.dot(a, b, preferred_element_type=F32, **kw)


def iota(shape, axis):
    return lax.broadcasted_iota(jnp.int32, shape, axis)


def kernel(
    n, nb, cap, lists,
    plen, slen, codes, q, kv, pool, x, b_t, b_rows, c_rows, dt, rate, skip, prior,
    attn_o, ssm_o,
    tiles, combs, sendbuf, recv, qbuf, kbuf, vbuf, mbuf, lbuf, accbuf, obuf,
    lx, dx, l_t, dt_t, sbuf, ybuf, hin, hout,
    ts, tr, cs, cr, ps, pr, qs, qr, ks, kr, vs, vr, os, orr, hs, hr,
):
    me = lax.axis_index("cache")
    j = lax.axis_index("blk")
    tok = x.shape[0]
    width = GROUP * HD
    prefix_limit = plen[0]
    suffix_limit = slen[0]

    def zpeer(d):
        return lax.rem(me + d, n)

    def bpeer(e):
        return lax.rem(j + e, nb)

    barrier = pltpu.get_barrier_semaphore()

    def greet_z(d, carry):
        pl.semaphore_signal(barrier, inc=1, device_id={"cache": zpeer(d)}, device_id_type=pl.DeviceIdType.MESH)
        return carry

    def greet_b(e, carry):
        pl.semaphore_signal(barrier, inc=1, device_id={"blk": bpeer(e)}, device_id_type=pl.DeviceIdType.MESH)
        return carry

    lax.fori_loop(1, n, greet_z, 0)
    lax.fori_loop(1, nb, greet_b, 0)
    pl.semaphore_wait(barrier, n - 1 + nb - 1)

    def tile_copy(e):
        return remote(codes, tiles.at[j], ts.at[e], tr.at[e], {"blk": bpeer(e)})

    def q_copy(e):
        to = bpeer(e)
        return remote(q.at[:, pl.ds(pl.multiple_of(to * width, width), width)], qbuf.at[j], qs.at[e], qr.at[e], {"blk": to})

    def k_copy(e):
        to = bpeer(e)
        return remote(kv.at[:, pl.ds(pl.multiple_of(to * HD, HD), HD)], kbuf.at[j], ks.at[e], kr.at[e], {"blk": to})

    def v_copy(e):
        to = bpeer(e)
        return remote(kv.at[:, pl.ds(pl.multiple_of(KVH * HD + to * HD, HD), HD)], vbuf.at[j], vs.at[e], vr.at[e], {"blk": to})

    def comb_copy(d):
        return remote(combs.at[0], combs.at[d], cs.at[d], cr.at[d], {"cache": zpeer(d)})

    def page_copy(d):
        return remote(sendbuf.at[d], recv.at[d], ps.at[d], pr.at[d], {"cache": zpeer(d)})

    def state_copy():
        return remote(hout, hin, hs, hr, {"blk": bpeer(1)})

    def out_copy(e):
        to = bpeer(e)
        return remote(obuf.at[to], attn_o.at[:, pl.ds(pl.multiple_of(j * width, width), width)], os.at[e], orr.at[e], {"blk": to})

    def each_b(what):
        def body(e, carry):
            what(e)
            return carry
        lax.fori_loop(1, nb, body, 0)

    def each_z(what, low=1, high=n):
        def body(d, carry):
            what(d)
            return carry
        lax.fori_loop(low, high, body, 0)

    each_b(lambda e: tile_copy(e).start())
    each_b(lambda e: (q_copy(e).start(), k_copy(e).start(), v_copy(e).start()))
    tiles[j] = codes[...]
    each_b(lambda e: tile_copy(e).wait_recv())
    combs[0] = jnp.sum(tiles[...], axis=0)
    each_z(lambda d: comb_copy(d).start())
    qbuf[j] = q[:, pl.ds(pl.multiple_of(j * width, width), width)]
    kbuf[j] = kv[:, pl.ds(pl.multiple_of(j * HD, HD), HD)]
    vbuf[j] = kv[:, pl.ds(pl.multiple_of(KVH * HD + j * HD, HD), HD)]

    lanes = combs.shape[2]
    before = jnp.where(iota((lanes, lanes), 0) < iota((lanes, lanes), 1), 1.0, 0.0).astype(BF16)

    def placing(slot, owner):
        named = combs[slot, 0:1, :] == owner + 1
        flags = jnp.broadcast_to(jnp.where(named, 1.0, 0.0), (16, lanes)).astype(BF16)
        rank = nn(flags, before)[0:1].astype(jnp.int32)
        return jnp.where((rank == iota((cap, lanes), 0)) & named, 1.0, 0.0).astype(BF16)

    def packed(slot):
        spots = pool.shape[0]
        wants = jnp.where(combs[slot, 1:2, :] == iota((spots, lanes), 0), 1.0, 0.0).astype(BF16)
        chosen = nt(placing(slot, me), wants).astype(BF16)
        return nn(chosen, pool[...]).astype(BF16)

    def answer(d):
        comb_copy(d).wait_recv()
        back = n - d
        sendbuf[back] = packed(d)
        page_copy(back).start()

    each_z(answer)
    recv[0] = packed(0)

    tri = jnp.where(iota((tok, tok), 0) >= iota((tok, tok), 1), 1.0, 0.0)
    exact = dict(precision=lax.Precision.HIGHEST)
    spread = jnp.where(iota((SH, SH * HP), 0) == iota((SH, SH * HP), 1) // HP, 1.0, 0.0)
    logs = nn(tri, dt[...] * (-rate[...]), **exact)
    lx[...] = nn(logs, spread, **exact)
    dx[...] = nn(dt[...], spread, **exact)
    l_t[...] = logs.T
    dt_t[...] = dt[...].T
    gram = nt(c_rows[...], b_rows[...])
    lower = iota((tok, tok), 0) >= iota((tok, tok), 1)
    first_half = iota((tok, 2 * HP), 1) < HP

    def pair_local(pair, carry):
        at = pl.ds(pl.multiple_of(pair * 2 * HP, 2 * HP), 2 * HP)
        xs = x[:, at]
        xf = xs.astype(F32)
        ltile = lx[:, at]

        def mixed(which):
            column = ltile[:, which * HP : which * HP + 1]
            row = l_t[pl.ds(2 * pair + which, 1), :]
            step = dt_t[pl.ds(2 * pair + which, 1), :]
            decay = jnp.exp(jnp.where(lower, column - row, NEG))
            return nn((gram * decay * step).astype(BF16), xs)

        ybuf[:, at] = jnp.where(first_half, mixed(0), mixed(1)) + skip[:, at] * xf
        scaled = (jnp.exp(ltile[tok - 1 : tok] - ltile) * dx[:, at] * xf).astype(BF16)
        sbuf[:, at] = nn(b_t[...], scaled)
        return carry

    lax.fori_loop(0, SH // 2, pair_local, 0)

    def chain():
        @pl.when(j == 0)
        def _():
            def fill(pair, carry):
                at = pl.ds(pl.multiple_of(pair * 2 * HP, 2 * HP), 2 * HP)
                hin[:, at] = prior[at, :].T.astype(BF16)
                return carry
            lax.fori_loop(0, SH // 2, fill, 0)

        @pl.when(j > 0)
        def _():
            state_copy().wait_recv()

        def onward(pair, carry):
            at = pl.ds(pl.multiple_of(pair * 2 * HP, 2 * HP), 2 * HP)
            decay = jnp.exp(lx[tok - 1 : tok, at])
            hout[:, at] = (decay * hin[:, at].astype(F32) + sbuf[:, at]).astype(BF16)
            return carry

        @pl.when(j < nb - 1)
        def _():
            lax.fori_loop(0, SH // 2, onward, 0)
            state_copy().start()

        alive = j * tok + iota((tok, 2 * HP), 0) < suffix_limit

        def read(pair, carry):
            at = pl.ds(pl.multiple_of(pair * 2 * HP, 2 * HP), 2 * HP)
            total = ybuf[:, at] + jnp.exp(lx[:, at]) * nn(c_rows[...], hin[:, at])
            ssm_o[:, at] = jnp.where(alive, total, 0.0).astype(BF16)
            return carry

        lax.fori_loop(0, SH // 2, read, 0)

    scale = 1.0 / math.sqrt(HD)
    rows = GROUP * tok

    def attend(b, keys, values, seen, first=False, last=False):
        qb = jnp.concatenate([qbuf[b, :, h * HD : (h + 1) * HD] for h in range(GROUP)], axis=0)
        scores = jnp.where(seen, nt(qb, keys) * scale, NEG)
        top = jnp.max(scores, axis=1, keepdims=True)
        if not first:
            old = mbuf[b]
            top = jnp.maximum(top, old)
            factor = jnp.exp(old - top)
        weights = jnp.exp(scores - top)
        total = jnp.sum(weights, axis=1, keepdims=True)
        mixed = nn(weights.astype(BF16), values)
        if not first:
            total = total + lbuf[b] * factor
            mixed = mixed + accbuf[b] * factor
        if not last:
            mbuf[b] = top
            lbuf[b] = total
            accbuf[b] = mixed
            return None
        alive = b * tok + lax.rem(iota((rows, HD), 0), tok) < suffix_limit
        return jnp.where(alive, mixed / total, 0.0).astype(BF16)

    each_b(lambda e: (q_copy(e).wait_recv(), k_copy(e).wait_recv(), v_copy(e).wait_recv()))

    def suffix_phase():
        keys = kbuf[...].reshape(nb * tok, HD)
        values = vbuf[...].reshape(nb * tok, HD)

        def block(b, carry):
            where_q = b * tok + lax.rem(iota((rows, nb * tok), 0), tok)
            where_k = iota((rows, nb * tok), 1)
            attend(b, keys, values, (where_k <= where_q) & (where_k < suffix_limit), first=True)
            return carry

        lax.fori_loop(0, nb, block, 0)

    per = max(1, n // 4)
    groups = n // per
    order = [0, 1, 3, 2] if groups == 4 else list(range(groups))

    def page_phase(g, last):
        if g == 0:
            each_z(lambda d: page_copy(d).wait_recv(), 1, per)
        else:
            each_z(lambda d: page_copy(d).wait_recv(), g * per, (g + 1) * per)
        span = per * cap
        slots = [lax.rem(me - d + n, n) for d in range(g * per, (g + 1) * per)]
        place = jnp.concatenate([placing(0, o) for o in slots], axis=0)
        k = iota((16, lanes), 1)
        number = lax.rem(k, lists) * nb + k // lists + 1
        page = nt(number.astype(F32).astype(BF16), jnp.concatenate([place] * PAGE, axis=0))[0:1].astype(jnp.int32)
        offset = iota((1, PAGE * span), 1) // span
        seen = (page > 0) & ((page - 1) * PAGE + offset < prefix_limit)

        def part(low):
            return jnp.concatenate(
                [
                    recv[g * per : (g + 1) * per, :, low + i * HD : low + (i + 1) * HD].reshape(span, HD)
                    for i in range(PAGE)
                ],
                axis=0,
            )

        keys = part(0)
        values = part(PAGE * HD)

        def block(e, carry):
            b = bpeer(e)
            out = attend(b, keys, values, seen, last=last)
            if last:
                for h in range(GROUP):
                    obuf[b, :, h * HD : (h + 1) * HD] = out[h * tok : (h + 1) * tok]

                @pl.when(e < nb)
                def _():
                    out_copy(e).start()
            return carry

        lax.fori_loop(1, nb + 1, block, 0)

    for phase in range(groups + 1):
        if phase < nb:
            pl.when(j == phase)(chain)
        if phase == 0:
            suffix_phase()
        else:
            page_phase(order[phase - 1], phase == groups)
    attn_o[:, pl.ds(pl.multiple_of(j * width, width), width)] = obuf[j]

    each_b(lambda e: out_copy(e).wait())
    each_b(lambda e: (tile_copy(e).wait_send(), q_copy(e).wait_send(), k_copy(e).wait_send(), v_copy(e).wait_send()))
    each_z(lambda d: (comb_copy(d).wait_send(), page_copy(d).wait_send()))

    @pl.when(j < nb - 1)
    def _():
        state_copy().wait_send()


def local(
    queries, kv_new, page_pool, page_owner, page_slot, prefix_len, suffix_len,
    ssm_in, b_in, c_in, step_size, decay_rate, skip_gain, prior_state,
):
    n = lax.axis_size("cache")
    nb = lax.axis_size("blk")
    j = lax.axis_index("blk")
    tok = queries.shape[1]
    lists = page_owner.shape[2]
    lanes = nb * lists
    cap = max(16, max(2, 2 * lists // n) * nb)
    half = KVH * HD
    pages = page_pool[0]
    spots = pages.shape[0]
    chosen = jnp.stack(
        [
            lax.dynamic_slice_in_dim(pages, j * HD, HD, 2),
            lax.dynamic_slice_in_dim(pages, half + j * HD, HD, 2),
        ],
        axis=1,
    ).reshape(spots, 2 * PAGE * HD)
    if spots < 128:
        chosen = jnp.pad(chosen, ((0, 128 - spots), (0, 0)))
    pair = jnp.stack([page_owner[0, 0, :, 0] + 1, page_slot[0, 0]])
    mine = jnp.arange(lanes, dtype=jnp.int32) // lists == j
    codes = jnp.where(mine[None], jnp.tile(pair, (1, nb)), 0)
    codes = jnp.pad(codes, ((0, 6), (0, 0)))
    vmem = pl.BlockSpec(memory_space=pltpu.VMEM)
    smem = pl.BlockSpec(memory_space=pltpu.SMEM)
    dma = pltpu.SemaphoreType.DMA
    wide = SH * HP
    rows = GROUP * tok
    attn, ssm = pl.pallas_call(
        functools.partial(kernel, n, nb, cap, lists),
        out_shape=(
            jax.ShapeDtypeStruct((tok, QH * HD), BF16),
            jax.ShapeDtypeStruct((tok, wide), BF16),
        ),
        in_specs=[smem, smem] + [vmem] * 12,
        out_specs=(vmem, vmem),
        scratch_shapes=[
            pltpu.VMEM((nb, 8, lanes), jnp.int32),
            pltpu.VMEM((n, 8, lanes), jnp.int32),
            pltpu.VMEM((n, cap, 2 * PAGE * HD), BF16),
            pltpu.VMEM((n, cap, 2 * PAGE * HD), BF16),
            pltpu.VMEM((nb, tok, GROUP * HD), BF16),
            pltpu.VMEM((nb, tok, HD), BF16),
            pltpu.VMEM((nb, tok, HD), BF16),
            pltpu.VMEM((nb, rows, 1), F32),
            pltpu.VMEM((nb, rows, 1), F32),
            pltpu.VMEM((nb, rows, HD), F32),
            pltpu.VMEM((nb, tok, GROUP * HD), BF16),
            pltpu.VMEM((tok, wide), F32),
            pltpu.VMEM((tok, wide), F32),
            pltpu.VMEM((SH, tok), F32),
            pltpu.VMEM((SH, tok), F32),
            pltpu.VMEM((NS, wide), F32),
            pltpu.VMEM((tok, wide), F32),
            pltpu.VMEM((NS, wide), BF16),
            pltpu.VMEM((NS, wide), BF16),
            dma((nb,)), dma((nb,)), dma((n,)), dma((n,)), dma((n,)), dma((n,)),
            dma((nb,)), dma((nb,)), dma((nb,)), dma((nb,)), dma((nb,)), dma((nb,)),
            dma((nb,)), dma((nb,)), dma, dma,
        ],
        compiler_params=pltpu.CompilerParams(
            collective_id=0, has_side_effects=True, vmem_limit_bytes=56 * 1024 * 1024
        ),
    )(
        prefix_len, suffix_len, codes, queries[0], kv_new[0], chosen, ssm_in[0],
        b_in[0].T, b_in[0], c_in[0], step_size[0], decay_rate[None, :],
        jnp.repeat(skip_gain, HP)[None, :], prior_state[0].reshape(wide, NS),
    )
    return attn[None], ssm[None]


def solution(mesh):
    in_specs = (
        P(("groups", "cache"), "blk", None),
        P(("groups", "cache"), "blk", None),
        P(("groups", "cache"), None, None, None),
        P(("groups", "cache"), "blk", None, None),
        P(("groups", "cache"), "blk", None),
        P(("groups", "cache")),
        P(("groups", "cache")),
        P(("groups", "cache"), "blk", None),
        P(("groups", "cache"), "blk", None),
        P(("groups", "cache"), "blk", None),
        P(("groups", "cache"), "blk", None),
        P(),
        P(),
        P(("groups", "cache"), None, None, None),
    )
    out_specs = (P(("groups", "cache"), "blk", None), P(("groups", "cache"), "blk", None))
    return jax.shard_map(local, mesh=mesh, in_specs=in_specs, out_specs=out_specs, check_vma=False)
```

time: 201 us -> 76.8 us (0.38)
  the two profiles are of different devices: /device:TPU:0 before, /device:TPU:21 now
where the time goes in v1:
time: 76.8 us; the launch traced here: 76.4 us
  Pallas kernels  62.2 us (81%)
  local copies, waits for them, and re-layouts  10.8 us (14%)
  between operations  1.96 us (3%)
  other arithmetic  1.43 us (2%)
    pallas_call x1, Pallas kernels, local(): pl.pallas_call(functools.partial(kernel, n, nb, cap, lists), out_shape=(j...  62.2 us
    unnamed x4, local copies, waits for them, and re-layouts  6.14 us

profile of v1, /device:TPU:21, one launch (start us, length us, event | category | flops | bytes accessed | tf_op | source)
XLA Modules:
  0.0 76.4 jit_solution(11796666695405188262)
XLA Ops:
  1.9 0.7 add_bitcast_fusion
  2.6 0.7 pad_add_fusion
  3.3 0.1 tile.10
  3.4 0.6 pad.4.codes
  4.0 0.7 broadcast_in_dim.28
  4.7 0.7 broadcast_in_dim_reshape.3.skip
  5.4 1.5 %copy.17.b_t = bf16[128,128]{1,0:T(8,128)(2,1)} copy(bf16[128,128]{0,1:T(8,128)(2,1)} %bitcast.33) | data formatting | bytes 65536 | tf_op jit(solution)/shard_map/transpose | solution.py:392
  6.8 1.4 %copy.16 = f32[1,128,32]{2,1,0:T(8,128)} copy(f32[1,128,32]{1,2,0:T(8,128)} %param.24) | data formatting | bytes 32768 | tf_op args[10]
  8.3 1.1 %dynamic-slice_bitcast_fusion.1 = (bf16[128,1,8,128]{3,2,1,0:T(8,128)(2,1)S(1)}, bf16[128,1,8,128]{3,2,1,0:T(8,128)(2,1)S(1)}) fusion(bf16[1,128,8,1024]{3,2,1,0:T(8,128)(2,1)} %param.16, s32[]{:T(128)S(6)} %select_n.21, s32[]{:T(128)S(6)} %select_n.22), kind=kLoop, calls=%fused_computation.3 | loop fusion | bytes 1048584 | tf_op jit(solution)/shard_map/stack | solution.py:337
  9.4 0.1 pad_maximum_fusion
  9.5 0.9 %copy.20 = bf16[16,8,16,128]{3,1,2,0:T(8,128)(2,1)} copy(bf16[16,8,16,128]{3,2,1,0:T(8,128)(2,1)S(1)} %bitcast.24) | data formatting | bytes 1048576
  10.4 62.2 %shard_map.149 = (bf16[128,2048]{1,0:T(8,128)(2,1)}, bf16[128,2048]{1,0:T(8,128)(2,1)}) custom-call(s32[1]{0:T(128)S(6)} %copy.23.plen, s32[1]{0:T(128)S(6)} %copy.24.slen, s32[8,128]{1,0:T(8,128)} %pad.4.codes, bf16[128,2048]{1,0:T(8,128)(2,1)} %bitcast.29, bf16[128,1024]{1,0:T(8,128)(2,1)} %bitcast.31, bf16[128,2048]{1,0:T(8,128)(2,1)} %bitcast.25, ...), custom_call_target="tpu_custom_call" | custom-call | tf_op jit(solution)/shard_map/pallas_call | solution.py:355
  72.6 1.9 %copy.25 = bf16[1,128,2048]{2,1,0:T(8,128)(2,1)} copy(bf16[1,128,2048]{2,1,0:T(8,128)(2,1)} %bitcast.28) | data formatting | bytes 1048576
  74.5 1.9 %copy.26 = bf16[1,128,2048]{2,1,0:T(8,128)(2,1)} copy(bf16[1,128,2048]{2,1,0:T(8,128)(2,1)} %bitcast.27) | data formatting | bytes 1048576
  (3 shorter events, 0.0 us)

commit v2 on v1

--- a/solution.py
+++ b/solution.py
@@ -46,10 +46,11 @@
 
 def kernel(
     n, nb, cap, lists,
-    plen, slen, codes, q, kv, pool, x, b_t, b_rows, c_rows, dt, rate, skip, prior,
+    plen, slen, owner, slot_row, q, kv, pages, x, b_rows, c_rows, step_t, rate, gain, prior_hbm,
     attn_o, ssm_o,
+    codes, pool, page_k, page_v, flat, prior, b_t, skip, load_sem,
     tiles, combs, sendbuf, recv, qbuf, kbuf, vbuf, mbuf, lbuf, accbuf, obuf,
-    lx, dx, l_t, dt_t, sbuf, ybuf, hin, hout,
+    lx, dx, l_t, sbuf, ybuf, hin, hout,
     ts, tr, cs, cr, ps, pr, qs, qr, ks, kr, vs, vr, os, orr, hs, hr,
 ):
     me = lax.axis_index("cache")
@@ -59,6 +60,16 @@
     prefix_limit = plen[0]
     suffix_limit = slen[0]
 
+    half = KVH * HD
+    key_load = pltpu.make_async_copy(pages.at[:, :, pl.ds(pl.multiple_of(j * HD, HD), HD)], page_k, load_sem.at[0])
+    value_load = pltpu.make_async_copy(pages.at[:, :, pl.ds(pl.multiple_of(half + j * HD, HD), HD)], page_v, load_sem.at[1])
+    prior_load = pltpu.make_async_copy(prior_hbm, prior, load_sem.at[2])
+    own_q = pltpu.make_async_copy(q.at[:, pl.ds(pl.multiple_of(j * width, width), width)], qbuf.at[j], load_sem.at[3])
+    own_k = pltpu.make_async_copy(kv.at[:, pl.ds(pl.multiple_of(j * HD, HD), HD)], kbuf.at[j], load_sem.at[4])
+    own_v = pltpu.make_async_copy(kv.at[:, pl.ds(pl.multiple_of(half + j * HD, HD), HD)], vbuf.at[j], load_sem.at[5])
+    for load in (key_load, value_load, prior_load, own_q, own_k, own_v):
+        load.start()
+
     def zpeer(d):
         return lax.rem(me + d, n)
 
@@ -77,6 +88,11 @@
 
     lax.fori_loop(1, n, greet_z, 0)
     lax.fori_loop(1, nb, greet_b, 0)
+    line = iota((16, lists), 0)
+    listed = jnp.where(line == 0, owner[...] + 1, jnp.where(line == 1, slot_row[...], 0))
+    lanes = nb * lists
+    spot = jnp.where(iota((lists, lanes), 0) + j * lists == iota((lists, lanes), 1), 1.0, 0.0)
+    codes[...] = nn(listed.astype(F32).astype(BF16), spot.astype(BF16))[0:8].astype(jnp.int32)
     pl.semaphore_wait(barrier, n - 1 + nb - 1)
 
     def tile_copy(e):
@@ -122,14 +138,18 @@
     each_b(lambda e: tile_copy(e).start())
     each_b(lambda e: (q_copy(e).start(), k_copy(e).start(), v_copy(e).start()))
     tiles[j] = codes[...]
+    spots = page_k.shape[0]
+    if spots < pool.shape[0]:
+        flat[...] = jnp.zeros_like(flat)
+    for which, load, held in ((0, key_load, page_k), (1, value_load, page_v)):
+        load.wait()
+        flat[0 : spots * PAGE] = held[...].astype(F32).reshape(spots * PAGE, HD)
+        for i in range(PAGE):
+            at = (which * PAGE + i) * HD
+            pool[:, at : at + HD] = flat[pl.ds(i, pool.shape[0], stride=PAGE), :].astype(BF16)
     each_b(lambda e: tile_copy(e).wait_recv())
     combs[0] = jnp.sum(tiles[...], axis=0)
     each_z(lambda d: comb_copy(d).start())
-    qbuf[j] = q[:, pl.ds(pl.multiple_of(j * width, width), width)]
-    kbuf[j] = kv[:, pl.ds(pl.multiple_of(j * HD, HD), HD)]
-    vbuf[j] = kv[:, pl.ds(pl.multiple_of(KVH * HD + j * HD, HD), HD)]
-
-    lanes = combs.shape[2]
     before = jnp.where(iota((lanes, lanes), 0) < iota((lanes, lanes), 1), 1.0, 0.0).astype(BF16)
 
     def placing(slot, owner):
@@ -156,11 +176,13 @@
     tri = jnp.where(iota((tok, tok), 0) >= iota((tok, tok), 1), 1.0, 0.0)
     exact = dict(precision=lax.Precision.HIGHEST)
     spread = jnp.where(iota((SH, SH * HP), 0) == iota((SH, SH * HP), 1) // HP, 1.0, 0.0)
-    logs = nn(tri, dt[...] * (-rate[...]), **exact)
+    dt = step_t[...].T
+    logs = nn(tri, dt * (-rate[...]), **exact)
     lx[...] = nn(logs, spread, **exact)
-    dx[...] = nn(dt[...], spread, **exact)
+    dx[...] = nn(dt, spread, **exact)
+    skip[...] = nn(jnp.broadcast_to(gain[...], (8, SH)), spread, **exact)
     l_t[...] = logs.T
-    dt_t[...] = dt[...].T
+    b_t[...] = b_rows[...].astype(F32).T.astype(BF16)
     gram = nt(c_rows[...], b_rows[...])
     lower = iota((tok, tok), 0) >= iota((tok, tok), 1)
     first_half = iota((tok, 2 * HP), 1) < HP
@@ -174,16 +196,18 @@
         def mixed(which):
             column = ltile[:, which * HP : which * HP + 1]
             row = l_t[pl.ds(2 * pair + which, 1), :]
-            step = dt_t[pl.ds(2 * pair + which, 1), :]
+            step = step_t[pl.ds(2 * pair + which, 1), :]
             decay = jnp.exp(jnp.where(lower, column - row, NEG))
             return nn((gram * decay * step).astype(BF16), xs)
 
-        ybuf[:, at] = jnp.where(first_half, mixed(0), mixed(1)) + skip[:, at] * xf
+        ybuf[:, at] = jnp.where(first_half, mixed(0), mixed(1)) + skip[0:1, at] * xf
         scaled = (jnp.exp(ltile[tok - 1 : tok] - ltile) * dx[:, at] * xf).astype(BF16)
         sbuf[:, at] = nn(b_t[...], scaled)
         return carry
 
     lax.fori_loop(0, SH // 2, pair_local, 0)
+
+    prior_load.wait()
 
     def chain():
         @pl.when(j == 0)
@@ -219,20 +243,20 @@
 
         lax.fori_loop(0, SH // 2, read, 0)
 
-    scale = 1.0 / math.sqrt(HD)
+    scale = math.log2(math.e) / math.sqrt(HD)
     rows = GROUP * tok
 
-    def attend(b, keys, values, seen, first=False, last=False):
+    def attend(b, keys, values_t, bias, first=False, last=False):
         qb = jnp.concatenate([qbuf[b, :, h * HD : (h + 1) * HD] for h in range(GROUP)], axis=0)
-        scores = jnp.where(seen, nt(qb, keys) * scale, NEG)
-        top = jnp.max(scores, axis=1, keepdims=True)
+        scores = nt(keys, qb) * scale + jnp.concatenate([bias] * GROUP, axis=1)
+        top = jnp.max(scores, axis=0, keepdims=True)
         if not first:
             old = mbuf[b]
             top = jnp.maximum(top, old)
-            factor = jnp.exp(old - top)
-        weights = jnp.exp(scores - top)
-        total = jnp.sum(weights, axis=1, keepdims=True)
-        mixed = nn(weights.astype(BF16), values)
+            factor = jnp.exp2(old - top)
+        weights = jnp.exp2(scores - top)
+        total = jnp.sum(weights, axis=0, keepdims=True)
+        mixed = nn(values_t, weights.astype(BF16))
         if not first:
             total = total + lbuf[b] * factor
             mixed = mixed + accbuf[b] * factor
@@ -241,19 +265,21 @@
             lbuf[b] = total
             accbuf[b] = mixed
             return None
-        alive = b * tok + lax.rem(iota((rows, HD), 0), tok) < suffix_limit
-        return jnp.where(alive, mixed / total, 0.0).astype(BF16)
-
+        return mixed * (1.0 / total)
+
+    for load in (own_q, own_k, own_v):
+        load.wait()
     each_b(lambda e: (q_copy(e).wait_recv(), k_copy(e).wait_recv(), v_copy(e).wait_recv()))
 
     def suffix_phase():
         keys = kbuf[...].reshape(nb * tok, HD)
-        values = vbuf[...].reshape(nb * tok, HD)
+        values_t = vbuf[...].reshape(nb * tok, HD).astype(F32).T.astype(BF16)
 
         def block(b, carry):
-            where_q = b * tok + lax.rem(iota((rows, nb * tok), 0), tok)
-            where_k = iota((rows, nb * tok), 1)
-            attend(b, keys, values, (where_k <= where_q) & (where_k < suffix_limit), first=True)
+            where_q = b * tok + iota((nb * tok, tok), 1)
+            where_k = iota((nb * tok, tok), 0)
+            seen = (where_k <= where_q) & (where_k < suffix_limit)
+            attend(b, keys, values_t, jnp.where(seen, 0.0, NEG), first=True)
             return carry
 
         lax.fori_loop(0, nb, block, 0)
@@ -270,11 +296,12 @@
         span = per * cap
         slots = [lax.rem(me - d + n, n) for d in range(g * per, (g + 1) * per)]
         place = jnp.concatenate([placing(0, o) for o in slots], axis=0)
-        k = iota((16, lanes), 1)
+        k = iota((lanes, tok), 0)
         number = lax.rem(k, lists) * nb + k // lists + 1
-        page = nt(number.astype(F32).astype(BF16), jnp.concatenate([place] * PAGE, axis=0))[0:1].astype(jnp.int32)
-        offset = iota((1, PAGE * span), 1) // span
+        page = nn(jnp.concatenate([place] * PAGE, axis=0), number.astype(F32).astype(BF16)).astype(jnp.int32)
+        offset = jnp.concatenate([jnp.full((span, tok), i, jnp.int32) for i in range(PAGE)], axis=0)
         seen = (page > 0) & ((page - 1) * PAGE + offset < prefix_limit)
+        bias = jnp.where(seen, 0.0, NEG)
 
         def part(low):
             return jnp.concatenate(
@@ -286,14 +313,16 @@
             )
 
         keys = part(0)
-        values = part(PAGE * HD)
+        values_t = part(PAGE * HD).astype(F32).T.astype(BF16)
 
         def block(e, carry):
             b = bpeer(e)
-            out = attend(b, keys, values, seen, last=last)
+            out = attend(b, keys, values_t, bias, last=last)
             if last:
+                alive = b * tok + iota((tok, HD), 0) < suffix_limit
                 for h in range(GROUP):
-                    obuf[b, :, h * HD : (h + 1) * HD] = out[h * tok : (h + 1) * tok]
+                    head = out[:, h * tok : (h + 1) * tok].T
+                    obuf[b, :, h * HD : (h + 1) * HD] = jnp.where(alive, head, 0.0).astype(BF16)
 
                 @pl.when(e < nb)
                 def _():
@@ -320,34 +349,29 @@
         state_copy().wait_send()
 
 
+def handed_on(attn, ssm, attn_out, ssm_out, sem):
+    first = pltpu.make_async_copy(attn, attn_out, sem.at[0])
+    second = pltpu.make_async_copy(ssm, ssm_out, sem.at[1])
+    first.start()
+    second.start()
+    first.wait()
+    second.wait()
+
+
 def local(
     queries, kv_new, page_pool, page_owner, page_slot, prefix_len, suffix_len,
     ssm_in, b_in, c_in, step_size, decay_rate, skip_gain, prior_state,
 ):
     n = lax.axis_size("cache")
     nb = lax.axis_size("blk")
-    j = lax.axis_index("blk")
     tok = queries.shape[1]
     lists = page_owner.shape[2]
     lanes = nb * lists
     cap = max(16, max(2, 2 * lists // n) * nb)
-    half = KVH * HD
-    pages = page_pool[0]
-    spots = pages.shape[0]
-    chosen = jnp.stack(
-        [
-            lax.dynamic_slice_in_dim(pages, j * HD, HD, 2),
-            lax.dynamic_slice_in_dim(pages, half + j * HD, HD, 2),
-        ],
-        axis=1,
-    ).reshape(spots, 2 * PAGE * HD)
-    if spots < 128:
-        chosen = jnp.pad(chosen, ((0, 128 - spots), (0, 0)))
-    pair = jnp.stack([page_owner[0, 0, :, 0] + 1, page_slot[0, 0]])
-    mine = jnp.arange(lanes, dtype=jnp.int32) // lists == j
-    codes = jnp.where(mine[None], jnp.tile(pair, (1, nb)), 0)
-    codes = jnp.pad(codes, ((0, 6), (0, 0)))
+    spots = page_pool.shape[1]
+    deep = max(128, spots)
     vmem = pl.BlockSpec(memory_space=pltpu.VMEM)
+    hbm = pl.BlockSpec(memory_space=pl.ANY)
     smem = pl.BlockSpec(memory_space=pltpu.SMEM)
     dma = pltpu.SemaphoreType.DMA
     wide = SH * HP
@@ -358,9 +382,18 @@
             jax.ShapeDtypeStruct((tok, QH * HD), BF16),
             jax.ShapeDtypeStruct((tok, wide), BF16),
         ),
-        in_specs=[smem, smem] + [vmem] * 12,
+        in_specs=[smem, smem, vmem, vmem, hbm, hbm, hbm] + [vmem] * 6 + [hbm],
         out_specs=(vmem, vmem),
         scratch_shapes=[
+            pltpu.VMEM((8, lanes), jnp.int32),
+            pltpu.VMEM((deep, 2 * PAGE * HD), BF16),
+            pltpu.VMEM((spots, PAGE, HD), BF16),
+            pltpu.VMEM((spots, PAGE, HD), BF16),
+            pltpu.VMEM((deep * PAGE, HD), F32),
+            pltpu.VMEM((wide, NS), F32),
+            pltpu.VMEM((NS, tok), BF16),
+            pltpu.VMEM((8, wide), F32),
+            dma((6,)),
             pltpu.VMEM((nb, 8, lanes), jnp.int32),
             pltpu.VMEM((n, 8, lanes), jnp.int32),
             pltpu.VMEM((n, cap, 2 * PAGE * HD), BF16),
@@ -368,13 +401,12 @@
             pltpu.VMEM((nb, tok, GROUP * HD), BF16),
             pltpu.VMEM((nb, tok, HD), BF16),
             pltpu.VMEM((nb, tok, HD), BF16),
-            pltpu.VMEM((nb, rows, 1), F32),
-            pltpu.VMEM((nb, rows, 1), F32),
-            pltpu.VMEM((nb, rows, HD), F32),
+            pltpu.VMEM((nb, 1, rows), F32),
+            pltpu.VMEM((nb, 1, rows), F32),
+            pltpu.VMEM((nb, HD, rows), F32),
             pltpu.VMEM((nb, tok, GROUP * HD), BF16),
             pltpu.VMEM((tok, wide), F32),
             pltpu.VMEM((tok, wide), F32),
-            pltpu.VMEM((SH, tok), F32),
             pltpu.VMEM((SH, tok), F32),
             pltpu.VMEM((NS, wide), F32),
             pltpu.VMEM((tok, wide), F32),
@@ -388,10 +420,20 @@
             collective_id=0, has_side_effects=True, vmem_limit_bytes=56 * 1024 * 1024
         ),
     )(
-        prefix_len, suffix_len, codes, queries[0], kv_new[0], chosen, ssm_in[0],
-        b_in[0].T, b_in[0], c_in[0], step_size[0], decay_rate[None, :],
-        jnp.repeat(skip_gain, HP)[None, :], prior_state[0].reshape(wide, NS),
+        prefix_len, suffix_len, page_owner.reshape(1, lists), page_slot.reshape(1, lists),
+        queries[0], kv_new[0], page_pool[0], ssm_in[0], b_in[0], c_in[0], step_size[0].T,
+        decay_rate[None, :], skip_gain[None, :], prior_state[0].reshape(wide, NS),
     )
+    attn, ssm = pl.pallas_call(
+        handed_on,
+        out_shape=(
+            jax.ShapeDtypeStruct(attn.shape, BF16),
+            jax.ShapeDtypeStruct(ssm.shape, BF16),
+        ),
+        in_specs=[hbm, hbm],
+        out_specs=(hbm, hbm),
+        scratch_shapes=[dma((2,))],
+    )(attn, ssm)
     return attn[None], ssm[None]
 
 

time: 76.8 us -> 86.2 us (1.12)
  Pallas kernels: 62.2 us -> 84 us
  local copies, waits for them, and re-layouts: 10.8 us -> 0 us
  other arithmetic: 1.43 us -> 0 us
    pallas_call x0 -> x1, Pallas kernels: none -> 32.9 us  [local(): pl.pallas_call(handed_on, out_shape=(jax.ShapeDtypeStruct(attn.shape, BF1...]
    pallas_call x1, Pallas kernels: 62.2 us -> 51.1 us  [local(): pl.pallas_call(functools.partial(kernel, n, nb, cap, lists), out_shape=(j...]
    unnamed x4 -> x0, local copies, waits for them, and re-layouts: 6.14 us -> none
    another operation x4 -> x0, local copies, waits for them, and re-layouts: 1.85 us -> none  [the longest x1 1.07 us: local(): jnp.stack([lax.dynamic_slice_in_dim(pages, j * HD, HD, 2), lax.dynamic_sl...]
    transpose x1 -> x0, local copies, waits for them, and re-layouts: 1.47 us -> none  [local(): b_in[0]]
where the time goes in v2:
time: 86.2 us; the launch traced here: 86 us
  Pallas kernels  84 us (97%)
  between operations  1.93 us (2%)
    pallas_call x1, Pallas kernels, local(): pl.pallas_call(functools.partial(kernel, n, nb, cap, lists), out_shape=(j...  51.1 us
    pallas_call x1, Pallas kernels, local(): pl.pallas_call(handed_on, out_shape=(jax.ShapeDtypeStruct(attn.shape, BF1...  32.9 us

profile of v2, /device:TPU:21, one launch (start us, length us, event | category | flops | bytes accessed | tf_op | source)
XLA Modules:
  0.0 86.0 jit_solution(4130839208499514718)
XLA Ops:
  1.9 51.1 %shard_map.149 = (bf16[128,2048]{1,0:T(8,128)(2,1)}, bf16[128,2048]{1,0:T(8,128)(2,1)}) custom-call(s32[1]{0:T(128)S(6)} %copy.16.plen, s32[1]{0:T(128)S(6)} %copy.17.slen, s32[1,32]{1,0:T(1,128)} %bitcast.24, s32[1,32]{1,0:T(1,128)} %bitcast.25, bf16[128,2048]{1,0:T(8,128)(2,1)} %bitcast.18, bf16[128,1024]{1,0:T(8,128)(2,1)} %bitcast.20, ...), custom_call_target="tpu_custom_call" | custom-call | tf_op jit(solution)/shard_map/pallas_call | solution.py:379
  53.1 32.9 %shard_map.150 = (bf16[128,2048]{1,0:T(8,128)(2,1)}, bf16[128,2048]{1,0:T(8,128)(2,1)}) custom-call(bf16[128,2048]{1,0:T(8,128)(2,1)} %get-tuple-element.6.attn, bf16[128,2048]{1,0:T(8,128)(2,1)} %get-tuple-element.7.ssm), custom_call_target="tpu_custom_call" | custom-call | tf_op jit(solution)/shard_map/pallas_call | solution.py:427
